TPU v7x, 256 devices: a whole 4x4x8 slice. The times are simulated.
256 devices in a mesh: ctx: 32 (over x, z), tp: 8 (over y, core).
Axes of the slice: x: 4, y: 4, z: 8, core: 2. Of those that a mesh axis runs over, the one named last changes fastest.
Arguments:
- queries: bfloat16 [16384, 8192], P('ctx', 'tp'), may hold values from -96 to 96
- keys: bfloat16 [16384, 1024], P(('ctx', 'tp')), may hold values from -6 to 6
- values: bfloat16 [16384, 1024], P(('ctx', 'tp')), may hold values from -6 to 6
- block_bound: int32 [64], replicated, may hold values from 0 to 256, as said below
- block_home: int32 [64], replicated, may hold values from 0 to 63, as said below
- pair_query: int32 [32, 32], P('ctx'), may hold values from -1 to 63, as said below
- pair_key: int32 [32, 32], P('ctx'), may hold values from -1 to 63, as said below
Outputs:
- attended: bfloat16 [16384, 8192], P('ctx', 'tp')
Inputs may be any that keep to these rules, and one draw needn't show every extreme that they name: `block_bound`: 256 marks a block without a document start; each aligned run of 8 logical blocks holds exactly one block with a value below 256. `block_home`: a permutation of 0 to 63. `pair_query`: over all workers, the listed pairs are exactly the pairs (q, k) of logical blocks with k <= q such that some token of q may see some token of k, each once; k >= q - 2 * 8 + 1; the pairs of worker w have query blocks whose owner is w - j mod 32 with 0 <= j < 4; the listed slots of a worker come first and the others hold -1. `pair_key`: the key block of the same slot, -1 exactly where pair_query is -1.
All inputs are finite; a program needn't handle non-finite values.
Results may differ from a plain program's by a relative error of at most 0.0048.
Values may be sent and summed in bfloat16 or wider, within the bound.
No kernel may reach another device: no remote copies, remote signals or barrier semaphores. Data moves between devices by JAX's collectives and lax.ppermute only.
A program may use at most 64 MiB of HBM per device.

v0:
```python
import functools

import jax
import jax.numpy as jnp
from jax import lax
from jax.experimental import pallas as pl
from jax.experimental.pallas import tpu as pltpu
from jax.sharding import PartitionSpec as P

HEAD_DIM = 128
BLK = 256
BPD = 2
NB = 64
GROUP = 8
NX, NZ = 4, 8
BACK = 16
NEG = -1e30
RT = 128
UNROLL = 8
COST = 300 * 1000 * 1000
SCALE = HEAD_DIM ** (-0.5) * 1.4426950408889634


def moved(block, dx, dz):
    route = [
        (x * NZ + z, (x + dx) % NX * NZ + (z + dz) % NZ)
        for x in range(NX)
        for z in range(NZ)
    ]
    return lax.ppermute(block, "ctx", route)


def chain(block, dx, dz, steps):
    out = []
    for _ in range(steps):
        block = moved(block, dx, dz)
        out.append(block)
    return out


def gather_blocks(own, work):
    up = chain(own, 0, 1, 3)
    down = chain(own, 0, -1, 4)
    right = chain(own, 1, 0, 2)
    left = chain(own, -1, 0, 1)
    both = lambda dx, dz: [(dx, dz, 0), (dx, dz, 1)]
    early = [(own, both(0, 0))]
    early += [(v, both(0, -i - 1)) for i, v in enumerate(up)]
    early += [(v, both(0, i + 1)) for i, v in enumerate(down[:3])]
    early += [(v, both(-i - 1, 0)) for i, v in enumerate(right)]
    early += [(v, both(i + 1, 0)) for i, v in enumerate(left)]
    first = jnp.concatenate([right[0][:1], left[0][:1], right[1][:1]])
    ahead = chain(first, 0, 1, 4)
    back = chain(first, 0, -1, 3)
    ahead = [(v, [(dx, -i - 1, 0) for dx in (-1, 1, -2)]) for i, v in enumerate(ahead)]
    back = [(v, [(dx, i + 1, 0) for dx in (-1, 1, -2)]) for i, v in enumerate(back)]
    middle, late = [(down[3], both(0, 4))] + ahead[:-1] + back[:-1], [ahead[-1], back[-1]]
    state = work(early)
    near = jnp.concatenate([up[0][1:], down[0][1:], up[1][1:], down[1][1:]])
    far = jnp.concatenate([up[2][1:], down[2][1:], down[3][1:]])
    far, state = lax.optimization_barrier((far, state))
    for lump, dzs, n_right, n_left in ((near, (-1, 1, -2, 2), 1, 2), (far, (-3, 3, 4), 2, 1)):
        for step, n in ((1, n_right), (-1, n_left)):
            for i, v in enumerate(chain(lump, step, 0, n)):
                hop_on = i + 1 < n or (n == 1 and len(dzs) == 4)
                (middle if hop_on else late).append((v, [(-step * (i + 1), dz, 1) for dz in dzs]))
    return state, middle, late


def attend_kernel(places, opening, closing, unroll, home_ref, bound_ref, q_ref, *refs):
    n_bufs = len(places)
    bufs, rest = refs[:n_bufs], refs[n_bufs:]
    if opening:
        inv, *rest = rest
    else:
        inv, rest = rest[0], rest[4:]
    m_ref, l_ref, acc_ref, *rest = rest
    if closing:
        o_ref, *rest = rest
    kv, lid, cnt, sem = rest
    me = lax.axis_index("ctx")
    my_x, my_z = me // NZ, me & (NZ - 1)
    of_x = {dx: ((my_x + dx) & (NX - 1)) * (NZ * BPD) for dx in (-2, -1, 0, 1, 2)}
    of_z = {dz: ((my_z + dz) & (NZ - 1)) * BPD for dz in range(-4, 5)}

    if opening:

        @pl.loop(0, NB)
        def _(b):
            inv[home_ref[b]] = b

        for qb in range(BPD):
            block = inv[me * BPD + qb]

            def earlier(i, first):
                at = block - 1 - i
                hit = (at >= 0) & (first < 0) & (bound_ref[jnp.maximum(at, 0)] < BLK)
                return jnp.where(hit, at, first)

            first = lax.fori_loop(0, BACK, earlier, jnp.int32(-1))
            first = jnp.where(bound_ref[block] == 0, block, jnp.maximum(first, 0))
            inv[NB + qb] = block
            inv[NB + BPD + qb] = first

    blocks = [inv[NB + qb] for qb in range(BPD)]
    firsts = [inv[NB + BPD + qb] for qb in range(BPD)]
    for qb in range(BPD):
        cnt[qb] = 0

    def fetch(src, qb, slot):
        return pltpu.make_async_copy(src, kv.at[qb, slot], sem.at[qb, slot])

    def list_slot(qb, logical):
        slot = cnt[qb]
        lid[qb, slot] = logical
        cnt[qb] = slot + 1
        return slot

    if opening:
        for qb in range(BPD):
            fetch(bufs[0].at[qb], qb, list_slot(qb, blocks[qb])).start()

    for buf, spots in zip(bufs, places):
        for i, (dx, dz, b) in enumerate(spots):
            logical = inv[of_x[dx] + of_z[dz] + b]
            for qb in range(BPD):

                @pl.when((logical >= firsts[qb]) & (logical < blocks[qb]))
                def _():
                    fetch(buf.at[i], qb, list_slot(qb, logical)).start()

    @pl.loop(0, BPD)
    def _(qb):
        block, first = inv[NB + qb], inv[NB + BPD + qb]
        top_row = pl.multiple_of(qb * BLK, BLK)
        bound = bound_ref[block]
        first_bound = bound_ref[first]
        doc_start = first * BLK + jnp.where((first < block) & (first_bound < BLK), first_bound, 0)
        row = lax.broadcasted_iota(jnp.int32, (BLK, 1), 0)
        low = jnp.where(row < bound, doc_start, block * BLK + bound)
        high = row + block * BLK

        def allowed(ids):
            col = lax.broadcasted_iota(jnp.int32, (1, BLK), 1)
            at = jnp.concatenate([col + i * BLK for i in ids], 1)
            return (at >= low) & (at <= high)

        def step(slots, ids, masked, fresh):
            keys = jnp.concatenate([kv[qb, s, :, 0].reshape(BLK, HEAD_DIM) for s in slots])
            vals = jnp.concatenate([kv[qb, s, :, 1].reshape(BLK, HEAD_DIM) for s in slots])
            n = len(slots) * BLK // HEAD_DIM
            vals = jnp.concatenate([vals, jnp.ones_like(vals)], 1)
            mask = allowed(ids) if masked else None

            def one_head(h):
                lanes = pl.ds(pl.multiple_of(h * HEAD_DIM, HEAD_DIM), HEAD_DIM)
                for r in range(0, BLK, RT):
                    at = (qb * GROUP + h, pl.ds(r, RT))
                    q = q_ref[pl.ds(top_row + r, RT), lanes]
                    s = lax.dot_general(
                        q, keys, (((1,), (1,)), ((), ())), preferred_element_type=jnp.float32
                    )
                    if masked:
                        s = jnp.where(mask[r : r + RT], s, NEG)
                    top = jnp.max(s, axis=1, keepdims=True)
                    if fresh:
                        top = jnp.broadcast_to(top, (RT, HEAD_DIM))
                    else:
                        before = m_ref[at]
                        top = jnp.maximum(before, top)
                        fade = jnp.exp2((before - top) * SCALE)
                    w = jnp.exp2((s - jnp.concatenate([top] * n, 1)) * SCALE)
                    pv = jnp.dot(
                        w.astype(jnp.bfloat16), vals, preferred_element_type=jnp.float32
                    )
                    m_ref[at] = top
                    if fresh:
                        l_ref[at] = pv[:, HEAD_DIM:]
                        acc_ref[at] = pv[:, :HEAD_DIM]
                    else:
                        l_ref[at] = l_ref[at] * fade + pv[:, HEAD_DIM:]
                        acc_ref[at] = acc_ref[at] * fade + pv[:, :HEAD_DIM]

            if unroll == GROUP:
                for h in range(GROUP):
                    one_head(h)
            else:

                @pl.loop(0, GROUP // unroll)
                def _(g):
                    for i in range(unroll):
                        one_head(g * unroll + i)

        def arrived(slot):
            fetch(bufs[0].at[0], qb, slot).wait()

        if opening:
            arrived(0)
            step([0], [block], True, True)
            base = 1
        else:
            base = 0
        seen = cnt[qb] - base

        @pl.loop(0, seen // 2)
        def _(c):
            slots = [base + 2 * c, base + 1 + 2 * c]
            for s in slots:
                arrived(s)
            ids = [lid[qb, s] for s in slots]
            edge = (bound < BLK) | (ids[0] == first) | (ids[1] == first)

            @pl.when(edge)
            def _():
                step(slots, ids, True, False)

            @pl.when(jnp.logical_not(edge))
            def _():
                step(slots, ids, False, False)

        @pl.when(seen % 2 == 1)
        def _():
            last = base + seen - 1
            arrived(last)
            step([last], [lid[qb, last]], True, False)

        if closing:
            for h in range(GROUP):
                at = qb * GROUP + h
                o_ref[pl.ds(top_row, BLK), h * HEAD_DIM : (h + 1) * HEAD_DIM] = (
                    acc_ref[at] / l_ref[at]
                ).astype(o_ref.dtype)


def attend(queries, block_bound, block_home, pieces, state=(), closing=True, unroll=UNROLL):
    bufs = [v for v, _ in pieces]
    places = [p for _, p in pieces]
    smem = pl.BlockSpec(memory_space=pltpu.SMEM)
    vmem = pl.BlockSpec(memory_space=pltpu.VMEM)
    stat = (BPD * GROUP, BLK, HEAD_DIM)
    n_blocks = sum(len(p) for p in places)
    out_shape = [jax.ShapeDtypeStruct(stat, jnp.float32)] * 3
    out_specs = [vmem] * 3
    table = [jax.ShapeDtypeStruct((NB + 2 * BPD,), jnp.int32)]
    if not state:
        out_shape, out_specs = table + out_shape, [smem] + out_specs
    if closing:
        out_shape = out_shape + [jax.ShapeDtypeStruct(queries.shape, queries.dtype)]
        out_specs = out_specs + [vmem]
    n_in = 3 + len(bufs)
    out = pl.pallas_call(
        functools.partial(attend_kernel, places, not state, closing, unroll),
        out_shape=out_shape,
        in_specs=[smem, smem, vmem]
        + [pl.BlockSpec(memory_space=pl.ANY)] * len(bufs)
        + ([smem] + [vmem] * 3 if state else []),
        out_specs=out_specs,
        input_output_aliases={n_in + 1 + i: i for i in range(3)} if state else {},
        scratch_shapes=[
            pltpu.VMEM((BPD, BACK, 4, 2, 64, HEAD_DIM), jnp.bfloat16),
            pltpu.SMEM((BPD, BACK), jnp.int32),
            pltpu.SMEM((BPD,), jnp.int32),
            pltpu.SemaphoreType.DMA((BPD, BACK)),
        ],
        cost_estimate=pl.CostEstimate(
            flops=n_blocks * COST, bytes_accessed=8 * 1024 * 1024, transcendentals=0
        ),
        compiler_params=pltpu.CompilerParams(vmem_limit_bytes=32 * 1024 * 1024),
    )(block_home, block_bound, queries, *bufs, *state)
    if closing:
        return out[-1]
    return out if not state else [state[0], *out]


def on_device(queries, keys, values, block_bound, block_home, pair_query, pair_key):
    rows = keys.shape[0]
    heads = keys.shape[1] // HEAD_DIM
    own = lax.all_to_all(
        jnp.concatenate([keys, values]), "tp", split_axis=1, concat_axis=0, tiled=True
    )
    own = own.reshape(BPD, heads // BPD, 2, rows, HEAD_DIM)
    args = (queries, block_bound, block_home)
    state, middle, late = gather_blocks(own, lambda pieces: attend(*args, pieces, closing=False))
    state = attend(*args, middle, state, closing=False)
    return attend(*args, late, state)


def solution(mesh):
    in_specs = (
        P("ctx", "tp"),
        P(("ctx", "tp"), None),
        P(("ctx", "tp"), None),
        P(),
        P(),
        P("ctx", None),
        P("ctx", None),
    )
    return jax.shard_map(
        on_device, mesh=mesh, in_specs=in_specs, out_specs=P("ctx", "tp"), check_vma=False
    )
```

profile of v0, /device:TPU:96, one launch (start us, length us, event | category | flops | bytes accessed | tf_op | source)
XLA Modules:
  0.0 93.6 jit_solution(17584780824115339446)
XLA Ops:
  0.0 1.0 %copy_bitcast_fusion = bf16[128,8,128]{2,0,1:T(8,128)(2,1)S(1)} fusion(bf16[64,1024]{1,0:T(8,128)(2,1)} %param.9, bf16[64,1024]{1,0:T(8,128)(2,1)} %param.8), kind=kLoop, calls=%fused_computation.3 | loop fusion | flops 524288 | bytes 524288 | tf_op jit(solution)/shard_map/all_to_all | solution.py:278
  1.0 0.0 copy-start
  1.0 0.0 copy-start.1
  1.0 0.0 copy-start.2
  1.1 11.9 %all_to_all.16 = bf16[128,8,128]{2,0,1:T(8,128)(2,1)S(1)} all-to-all(bf16[128,8,128]{2,0,1:T(8,128)(2,1)S(1)} %copy_bitcast_fusion), channel_id=1, replica_groups=mesh['ctx'=32,'tp'=8] {'tp'}, dimensions={1} | all-to-all | bytes 524288 | tf_op jit(solution)/shard_map/all_to_all | solution.py:278
  13.0 1.5 %collective-permute-start = (bf16[2,4,2,64,128]{4,3,2,1,0:T(8,128)(2,1)S(1)}, bf16[2,4,2,64,128]{4,3,2,1,0:T(8,128)(2,1)S(1)}, u32[]{:S(2)}, u32[]{:S(2)}) collective-permute-start(bf16[2,4,2,64,128]{4,3,2,1,0:T(8,128)(2,1)S(1)} %bitcast.8), channel_id=1, source_target_pairs={{0,64},{8,72},{16,80},{24,88},{32,96},{40,104},{48,112},{56,120},{... | collective-permute-start | bytes 786440 | tf_op jit(solution)/shard_map/ppermute | solution.py:30
  14.5 0.1 collective-permute-start.11
  14.6 3.1 %collective-permute-start.10 = (bf16[2,4,2,64,128]{4,3,2,1,0:T(8,128)(2,1)S(1)}, bf16[2,4,2,64,128]{4,3,2,1,0:T(8,128)(2,1)S(1)}, u32[]{:S(2)}, u32[]{:S(2)}) collective-permute-start(bf16[2,4,2,64,128]{4,3,2,1,0:T(8,128)(2,1)S(1)} %bitcast.10), channel_id=1, source_target_pairs={{0,8},{8,16},{16,24},{24,32},{32,40},{40,48},{48,56},{56,0},{64,72... | collective-permute-start | bytes 786440 | tf_op jit(solution)/shard_map/ppermute | solution.py:30
  17.7 1.7 %collective-permute-start.1 = (bf16[2,4,2,64,128]{4,3,2,1,0:T(8,128)(2,1)S(1)}, bf16[2,4,2,64,128]{4,3,2,1,0:T(8,128)(2,1)S(1)}, u32[]{:S(2)}, u32[]{:S(2)}) collective-permute-start(bf16[2,4,2,64,128]{4,3,2,1,0:T(8,128)(2,1)S(1)} %bitcast.11), channel_id=1, source_target_pairs={{0,192},{8,200},{16,208},{24,216},{32,224},{40,232},{48,240},{56,2... | collective-permute-start | bytes 786440 | tf_op jit(solution)/shard_map/ppermute | solution.py:30
  19.5 2.4 %collective-permute-done.refs_7_ = bf16[2,4,2,64,128]{4,3,2,1,0:T(8,128)(2,1)S(1)} collective-permute-done((bf16[2,4,2,64,128]{4,3,2,1,0:T(8,128)(2,1)S(1)}, bf16[2,4,2,64,128]{4,3,2,1,0:T(8,128)(2,1)S(1)}, u32[]{:S(2)}, u32[]{:S(2)}) %collective-permute-start) | collective-permute-done | bytes 262176 | tf_op jit(solution)/shard_map/ppermute | solution.py:30
  21.9 0.3 collective-permute-start.2
  22.2 1.1 %collective-permute-done.11.refs_4_ = bf16[2,4,2,64,128]{4,3,2,1,0:T(8,128)(2,1)S(1)} collective-permute-done((bf16[2,4,2,64,128]{4,3,2,1,0:T(8,128)(2,1)S(1)}, bf16[2,4,2,64,128]{4,3,2,1,0:T(8,128)(2,1)S(1)}, u32[]{:S(2)}, u32[]{:S(2)}) %collective-permute-start.11) | collective-permute-done | bytes 262176 | tf_op jit(solution)/shard_map/ppermute | solution.py:30
  23.3 0.0 collective-permute-start.13
  23.3 0.0 collective-permute-done.10.refs_1_
  23.3 3.2 %collective-permute-start.12 = (bf16[2,4,2,64,128]{4,3,2,1,0:T(8,128)(2,1)S(1)}, bf16[2,4,2,64,128]{4,3,2,1,0:T(8,128)(2,1)S(1)}, u32[]{:S(2)}, u32[]{:S(2)}) collective-permute-start(bf16[2,4,2,64,128]{4,3,2,1,0:T(8,128)(2,1)S(1)} %collective-permute-done.10.refs_1_), channel_id=1, source_target_pairs={{0,8},{8,16},{16,24},{24,32},{32,40},{40,48},{48,56},{56,0},{64,72... | collective-permute-start | bytes 786440 | tf_op jit(solution)/shard_map/ppermute | solution.py:30
  26.5 0.0 collective-permute-done.1.refs_9_
  26.6 3.3 %collective-permute-done.2.refs_8_ = bf16[2,4,2,64,128]{4,3,2,1,0:T(8,128)(2,1)S(1)} collective-permute-done((bf16[2,4,2,64,128]{4,3,2,1,0:T(8,128)(2,1)S(1)}, bf16[2,4,2,64,128]{4,3,2,1,0:T(8,128)(2,1)S(1)}, u32[]{:S(2)}, u32[]{:S(2)}) %collective-permute-start.2) | collective-permute-done | bytes 262176 | tf_op jit(solution)/shard_map/ppermute | solution.py:30
  29.9 3.2 %collective-permute-start.3 = (bf16[3,4,2,64,128]{4,3,2,1,0:T(8,128)(2,1)S(1)}, bf16[3,4,2,64,128]{4,3,2,1,0:T(8,128)(2,1)S(1)}, u32[]{:S(2)}, u32[]{:S(2)}) collective-permute-start(bf16[3,4,2,64,128]{4,3,2,1,0:T(8,128)(2,1)S(1)} %pad_maximum_fusion.1), channel_id=1, source_target_pairs={{0,8},{8,16},{16,24},{24,32},{32,40},{40,48},{48,56},{56,0},{64,72... | collective-permute-start | bytes 1179656 | tf_op jit(solution)/shard_map/ppermute | solution.py:30
  33.1 0.0 collective-permute-done.13.refs_5_
  33.1 0.0 collective-permute-start.17
  33.1 0.0 collective-permute-done.12.refs_2_
  33.1 3.2 %collective-permute-start.16 = (bf16[2,4,2,64,128]{4,3,2,1,0:T(8,128)(2,1)S(1)}, bf16[2,4,2,64,128]{4,3,2,1,0:T(8,128)(2,1)S(1)}, u32[]{:S(2)}, u32[]{:S(2)}) collective-permute-start(bf16[2,4,2,64,128]{4,3,2,1,0:T(8,128)(2,1)S(1)} %collective-permute-done.12.refs_2_), channel_id=1, source_target_pairs={{0,8},{8,16},{16,24},{24,32},{32,40},{40,48},{48,56},{56,0},{64,72... | collective-permute-start | bytes 786440 | tf_op jit(solution)/shard_map/ppermute | solution.py:30
  36.4 0.1 pad_maximum_fusion
  36.5 0.8 collective-permute-start.14
  37.3 1.3 %collective-permute-start.22 = (bf16[4,4,2,64,128]{4,3,2,1,0:T(8,128)(2,1)S(1)}, bf16[4,4,2,64,128]{4,3,2,1,0:T(8,128)(2,1)S(1)}, u32[]{:S(2)}, u32[]{:S(2)}) collective-permute-start(bf16[4,4,2,64,128]{4,3,2,1,0:T(8,128)(2,1)S(1)} %pad_maximum_fusion), channel_id=1, source_target_pairs={{0,64},{8,72},{16,80},{24,88},{32,96},{40,104},{48,112},{56,120},{... | collective-permute-start | bytes 1572872 | tf_op jit(solution)/shard_map/ppermute | solution.py:30
  38.6 2.1 %collective-permute-done.17.refs_6_ = bf16[2,4,2,64,128]{4,3,2,1,0:T(8,128)(2,1)S(1)} collective-permute-done((bf16[2,4,2,64,128]{4,3,2,1,0:T(8,128)(2,1)S(1)}, bf16[2,4,2,64,128]{4,3,2,1,0:T(8,128)(2,1)S(1)}, u32[]{:S(2)}, u32[]{:S(2)}) %collective-permute-start.17) | collective-permute-done | bytes 262176 | tf_op jit(solution)/shard_map/ppermute | solution.py:30
  40.7 4.2 %collective-permute-done.16.refs_3_ = bf16[2,4,2,64,128]{4,3,2,1,0:T(8,128)(2,1)S(1)} collective-permute-done((bf16[2,4,2,64,128]{4,3,2,1,0:T(8,128)(2,1)S(1)}, bf16[2,4,2,64,128]{4,3,2,1,0:T(8,128)(2,1)S(1)}, u32[]{:S(2)}, u32[]{:S(2)}) %collective-permute-start.16) | collective-permute-done | bytes 262176 | tf_op jit(solution)/shard_map/ppermute | solution.py:30
  44.9 0.0 collective-permute-done.3.refs_1_
  44.9 3.7 %collective-permute-start.4 = (bf16[3,4,2,64,128]{4,3,2,1,0:T(8,128)(2,1)S(1)}, bf16[3,4,2,64,128]{4,3,2,1,0:T(8,128)(2,1)S(1)}, u32[]{:S(2)}, u32[]{:S(2)}) collective-permute-start(bf16[3,4,2,64,128]{4,3,2,1,0:T(8,128)(2,1)S(1)} %collective-permute-done.3.refs_1_), channel_id=1, source_target_pairs={{0,8},{8,16},{16,24},{24,32},{32,40},{40,48},{48,56},{56,0},{64,72... | collective-permute-start | bytes 1179656 | tf_op jit(solution)/shard_map/ppermute | solution.py:30
  48.6 11.7 %shard_map.55 = (s32[68]{0:T(128)S(1)}, f32[16,256,128]{2,1,0:T(8,128)S(1)}, f32[16,256,128]{2,1,0:T(8,128)S(1)}, f32[16,256,128]{2,1,0:T(8,128)S(1)}) custom-call(s32[64]{0:T(128)S(1)} %copy-done.1, s32[64]{0:T(128)S(1)} %copy-done.2, bf16[512,1024]{1,0:T(8,128)(2,1)S(1)} %copy-done, bf16[2,4,2,64,128]{4,3,2,1,0:T(8,128)(2,1)S(1)} %bitcast.12, ...), custom_call_target="tpu_custom_call" | custom-call | flops 6000000000 | bytes 8388608 | tf_op jit(solution)/shard_map/pallas_call | solution.py:251
  60.4 0.0 collective-permute-done.7.refs_4_
  60.4 0.1 collective-permute-start.8
  60.5 0.0 collective-permute-done.18.refs_0_
  60.6 1.0 %collective-permute-start.19 = (bf16[3,4,2,64,128]{4,3,2,1,0:T(8,128)(2,1)S(1)}, bf16[3,4,2,64,128]{4,3,2,1,0:T(8,128)(2,1)S(1)}, u32[]{:S(2)}, u32[]{:S(2)}) collective-permute-start(bf16[3,4,2,64,128]{4,3,2,1,0:T(8,128)(2,1)S(1)} %pad_maximum_fusion.2), channel_id=1, source_target_pairs={{0,64},{8,72},{16,80},{24,88},{32,96},{40,104},{48,112},{56,120},{... | collective-permute-start | bytes 1179656 | tf_op jit(solution)/shard_map/ppermute | solution.py:30
  61.6 3.2 %collective-permute-start.5 = (bf16[3,4,2,64,128]{4,3,2,1,0:T(8,128)(2,1)S(1)}, bf16[3,4,2,64,128]{4,3,2,1,0:T(8,128)(2,1)S(1)}, u32[]{:S(2)}, u32[]{:S(2)}) collective-permute-start(bf16[3,4,2,64,128]{4,3,2,1,0:T(8,128)(2,1)S(1)} %collective-permute-done.4.refs_2_), channel_id=1, source_target_pairs={{0,8},{8,16},{16,24},{24,32},{32,40},{40,48},{48,56},{56,0},{64,72... | collective-permute-start | bytes 1179656 | tf_op jit(solution)/shard_map/ppermute | solution.py:30
  64.8 2.3 %collective-permute-start.15 = (bf16[4,4,2,64,128]{4,3,2,1,0:T(8,128)(2,1)S(1)}, bf16[4,4,2,64,128]{4,3,2,1,0:T(8,128)(2,1)S(1)}, u32[]{:S(2)}, u32[]{:S(2)}) collective-permute-start(bf16[4,4,2,64,128]{4,3,2,1,0:T(8,128)(2,1)S(1)} %collective-permute-done.14.refs_7_), channel_id=1, source_target_pairs={{0,192},{8,200},{16,208},{24,216},{32,224},{40,232},{48,240},{56,2... | collective-permute-start | bytes 1572872 | tf_op jit(solution)/shard_map/ppermute | solution.py:30
  67.1 0.1 collective-permute-start.21
  67.2 3.1 %collective-permute-done.8.refs_5_ = bf16[3,4,2,64,128]{4,3,2,1,0:T(8,128)(2,1)S(1)} collective-permute-done((bf16[3,4,2,64,128]{4,3,2,1,0:T(8,128)(2,1)S(1)}, bf16[3,4,2,64,128]{4,3,2,1,0:T(8,128)(2,1)S(1)}, u32[]{:S(2)}, u32[]{:S(2)}) %collective-permute-start.8) | collective-permute-done | bytes 393248 | tf_op jit(solution)/shard_map/ppermute | solution.py:30
  70.3 0.2 collective-permute-done.19.refs_8_
  70.5 1.0 %collective-permute-start.20 = (bf16[3,4,2,64,128]{4,3,2,1,0:T(8,128)(2,1)S(1)}, bf16[3,4,2,64,128]{4,3,2,1,0:T(8,128)(2,1)S(1)}, u32[]{:S(2)}, u32[]{:S(2)}) collective-permute-start(bf16[3,4,2,64,128]{4,3,2,1,0:T(8,128)(2,1)S(1)} %collective-permute-done.19.refs_8_), channel_id=1, source_target_pairs={{0,64},{8,72},{16,80},{24,88},{32,96},{40,104},{48,112},{56,120},{... | collective-permute-start | bytes 1179656 | tf_op jit(solution)/shard_map/ppermute | solution.py:30
  71.5 3.2 %collective-permute-start.6 = (bf16[3,4,2,64,128]{4,3,2,1,0:T(8,128)(2,1)S(1)}, bf16[3,4,2,64,128]{4,3,2,1,0:T(8,128)(2,1)S(1)}, u32[]{:S(2)}, u32[]{:S(2)}) collective-permute-start(bf16[3,4,2,64,128]{4,3,2,1,0:T(8,128)(2,1)S(1)} %collective-permute-done.5.refs_3_), channel_id=1, source_target_pairs={{0,8},{8,16},{16,24},{24,32},{32,40},{40,48},{48,56},{56,0},{64,72... | collective-permute-start | bytes 1179656 | tf_op jit(solution)/shard_map/ppermute | solution.py:30
  74.7 8.3 %shard_map.56 = (f32[16,256,128]{2,1,0:T(8,128)S(1)}, f32[16,256,128]{2,1,0:T(8,128)S(1)}, f32[16,256,128]{2,1,0:T(8,128)S(1)}) custom-call(s32[64]{0:T(128)S(1)} %copy-done.1, s32[64]{0:T(128)S(1)} %copy-done.2, bf16[512,1024]{1,0:T(8,128)(2,1)S(1)} %copy-done, ...), custom_call_target="tpu_custom_call", output_to_operand_aliasing={{0}: (13, {}), {1}: (14, {}), {2}: (15, {})} | custom-call | flops 8400000000 | bytes 8388608 | tf_op jit(solution)/shard_map/pallas_call | solution.py:251
  83.1 1.0 %collective-permute-done.21.refs_4_ = bf16[3,4,2,64,128]{4,3,2,1,0:T(8,128)(2,1)S(1)} collective-permute-done((bf16[3,4,2,64,128]{4,3,2,1,0:T(8,128)(2,1)S(1)}, bf16[3,4,2,64,128]{4,3,2,1,0:T(8,128)(2,1)S(1)}, u32[]{:S(2)}, u32[]{:S(2)}) %collective-permute-start.21) | collective-permute-done | bytes 393248 | tf_op jit(solution)/shard_map/ppermute | solution.py:30
  84.1 0.0 collective-permute-done.15.refs_2_
  84.1 0.0 collective-permute-done.9.refs_1_
  84.1 0.0 collective-permute-done.20.refs_3_
  84.1 0.0 collective-permute-done.6.refs_0_
  84.1 9.3 %shard_map.57 = (f32[16,256,128]{2,1,0:T(8,128)S(1)}, f32[16,256,128]{2,1,0:T(8,128)S(1)}, f32[16,256,128]{2,1,0:T(8,128)S(1)}, bf16[512,1024]{1,0:T(8,128)(2,1)}) custom-call(s32[64]{0:T(128)S(1)} %copy-done.1, s32[64]{0:T(128)S(1)} %copy-done.2, bf16[512,1024]{1,0:T(8,128)(2,1)S(1)} %copy-done, ...), custom_call_target="tpu_custom_call", output_to_operand_aliasing={{0}: (9, {}), {1}: (10, {}), {2}: (11, {})} | custom-call | flops 4800000000 | bytes 8388608 | tf_op jit(solution)/shard_map/pallas_call | solution.py:251
  (22 shorter events, 0.2 us)
Async XLA Ops:
  1.0 47.6 %copy-start = (bf16[512,1024]{1,0:T(8,128)(2,1)S(1)}, bf16[512,1024]{1,0:T(8,128)(2,1)}, u32[]{:S(2)}) copy-start(bf16[512,1024]{1,0:T(8,128)(2,1)} %q_ref.5) | copy-start | bytes 3145732
  1.0 47.6 %copy-start.1 = (s32[64]{0:T(128)S(1)}, s32[64]{0:T(128)}, u32[]{:S(2)}) copy-start(s32[64]{0:T(128)} %home_ref.5) | copy-start | bytes 772
  1.0 47.6 %copy-start.2 = (s32[64]{0:T(128)S(1)}, s32[64]{0:T(128)}, u32[]{:S(2)}) copy-start(s32[64]{0:T(128)} %bound_ref.5) | copy-start | bytes 772
  13.0 8.9 %collective-permute-start = (bf16[2,4,2,64,128]{4,3,2,1,0:T(8,128)(2,1)S(1)}, bf16[2,4,2,64,128]{4,3,2,1,0:T(8,128)(2,1)S(1)}, u32[]{:S(2)}, u32[]{:S(2)}) collective-permute-start(bf16[2,4,2,64,128]{4,3,2,1,0:T(8,128)(2,1)S(1)} %bitcast.8), channel_id=1, source_target_pairs={{0,64},{8,72},{16,80},{24,88},{32,96},{40,104},{48,112},{56,120},{... | collective-permute-start | bytes 786440 | tf_op jit(solution)/shard_map/ppermute | solution.py:30
  14.5 8.8 %collective-permute-start.11 = (bf16[2,4,2,64,128]{4,3,2,1,0:T(8,128)(2,1)S(1)}, bf16[2,4,2,64,128]{4,3,2,1,0:T(8,128)(2,1)S(1)}, u32[]{:S(2)}, u32[]{:S(2)}) collective-permute-start(bf16[2,4,2,64,128]{4,3,2,1,0:T(8,128)(2,1)S(1)} %bitcast.9), channel_id=1, source_target_pairs={{0,56},{8,0},{16,8},{24,16},{32,24},{40,32},{48,40},{56,48},{64,12... | collective-permute-start | bytes 786440 | tf_op jit(solution)/shard_map/ppermute | solution.py:30
  14.6 8.7 %collective-permute-start.10 = (bf16[2,4,2,64,128]{4,3,2,1,0:T(8,128)(2,1)S(1)}, bf16[2,4,2,64,128]{4,3,2,1,0:T(8,128)(2,1)S(1)}, u32[]{:S(2)}, u32[]{:S(2)}) collective-permute-start(bf16[2,4,2,64,128]{4,3,2,1,0:T(8,128)(2,1)S(1)} %bitcast.10), channel_id=1, source_target_pairs={{0,8},{8,16},{16,24},{24,32},{32,40},{40,48},{48,56},{56,0},{64,72... | collective-permute-start | bytes 786440 | tf_op jit(solution)/shard_map/ppermute | solution.py:30
  17.7 8.8 %collective-permute-start.1 = (bf16[2,4,2,64,128]{4,3,2,1,0:T(8,128)(2,1)S(1)}, bf16[2,4,2,64,128]{4,3,2,1,0:T(8,128)(2,1)S(1)}, u32[]{:S(2)}, u32[]{:S(2)}) collective-permute-start(bf16[2,4,2,64,128]{4,3,2,1,0:T(8,128)(2,1)S(1)} %bitcast.11), channel_id=1, source_target_pairs={{0,192},{8,200},{16,208},{24,216},{32,224},{40,232},{48,240},{56,2... | collective-permute-start | bytes 786440 | tf_op jit(solution)/shard_map/ppermute | solution.py:30
  21.9 8.0 %collective-permute-start.2 = (bf16[2,4,2,64,128]{4,3,2,1,0:T(8,128)(2,1)S(1)}, bf16[2,4,2,64,128]{4,3,2,1,0:T(8,128)(2,1)S(1)}, u32[]{:S(2)}, u32[]{:S(2)}) collective-permute-start(bf16[2,4,2,64,128]{4,3,2,1,0:T(8,128)(2,1)S(1)} %collective-permute-done.refs_7_), channel_id=1, source_target_pairs={{0,64},{8,72},{16,80},{24,88},{32,96},{40,104},{48,112},{56,120},{... | collective-permute-start | bytes 786440 | tf_op jit(solution)/shard_map/ppermute | solution.py:30
  23.3 9.9 %collective-permute-start.13 = (bf16[2,4,2,64,128]{4,3,2,1,0:T(8,128)(2,1)S(1)}, bf16[2,4,2,64,128]{4,3,2,1,0:T(8,128)(2,1)S(1)}, u32[]{:S(2)}, u32[]{:S(2)}) collective-permute-start(bf16[2,4,2,64,128]{4,3,2,1,0:T(8,128)(2,1)S(1)} %collective-permute-done.11.refs_4_), channel_id=1, source_target_pairs={{0,56},{8,0},{16,8},{24,16},{32,24},{40,32},{48,40},{56,48},{64,12... | collective-permute-start | bytes 786440 | tf_op jit(solution)/shard_map/ppermute | solution.py:30
  23.3 9.9 %collective-permute-start.12 = (bf16[2,4,2,64,128]{4,3,2,1,0:T(8,128)(2,1)S(1)}, bf16[2,4,2,64,128]{4,3,2,1,0:T(8,128)(2,1)S(1)}, u32[]{:S(2)}, u32[]{:S(2)}) collective-permute-start(bf16[2,4,2,64,128]{4,3,2,1,0:T(8,128)(2,1)S(1)} %collective-permute-done.10.refs_1_), channel_id=1, source_target_pairs={{0,8},{8,16},{16,24},{24,32},{32,40},{40,48},{48,56},{56,0},{64,72... | collective-permute-start | bytes 786440 | tf_op jit(solution)/shard_map/ppermute | solution.py:30
  29.9 15.0 %collective-permute-start.3 = (bf16[3,4,2,64,128]{4,3,2,1,0:T(8,128)(2,1)S(1)}, bf16[3,4,2,64,128]{4,3,2,1,0:T(8,128)(2,1)S(1)}, u32[]{:S(2)}, u32[]{:S(2)}) collective-permute-start(bf16[3,4,2,64,128]{4,3,2,1,0:T(8,128)(2,1)S(1)} %pad_maximum_fusion.1), channel_id=1, source_target_pairs={{0,8},{8,16},{16,24},{24,32},{32,40},{40,48},{48,56},{56,0},{64,72... | collective-permute-start | bytes 1179656 | tf_op jit(solution)/shard_map/ppermute | solution.py:30
  33.1 7.6 %collective-permute-start.17 = (bf16[2,4,2,64,128]{4,3,2,1,0:T(8,128)(2,1)S(1)}, bf16[2,4,2,64,128]{4,3,2,1,0:T(8,128)(2,1)S(1)}, u32[]{:S(2)}, u32[]{:S(2)}) collective-permute-start(bf16[2,4,2,64,128]{4,3,2,1,0:T(8,128)(2,1)S(1)} %collective-permute-done.13.refs_5_), channel_id=1, source_target_pairs={{0,56},{8,0},{16,8},{24,16},{32,24},{40,32},{48,40},{56,48},{64,12... | collective-permute-start | bytes 786440 | tf_op jit(solution)/shard_map/ppermute | solution.py:30
  33.1 11.8 %collective-permute-start.16 = (bf16[2,4,2,64,128]{4,3,2,1,0:T(8,128)(2,1)S(1)}, bf16[2,4,2,64,128]{4,3,2,1,0:T(8,128)(2,1)S(1)}, u32[]{:S(2)}, u32[]{:S(2)}) collective-permute-start(bf16[2,4,2,64,128]{4,3,2,1,0:T(8,128)(2,1)S(1)} %collective-permute-done.12.refs_2_), channel_id=1, source_target_pairs={{0,8},{8,16},{16,24},{24,32},{32,40},{40,48},{48,56},{56,0},{64,72... | collective-permute-start | bytes 786440 | tf_op jit(solution)/shard_map/ppermute | solution.py:30
  36.5 28.3 %collective-permute-start.14 = (bf16[4,4,2,64,128]{4,3,2,1,0:T(8,128)(2,1)S(1)}, bf16[4,4,2,64,128]{4,3,2,1,0:T(8,128)(2,1)S(1)}, u32[]{:S(2)}, u32[]{:S(2)}) collective-permute-start(bf16[4,4,2,64,128]{4,3,2,1,0:T(8,128)(2,1)S(1)} %pad_maximum_fusion), channel_id=1, source_target_pairs={{0,192},{8,200},{16,208},{24,216},{32,224},{40,232},{48,240},{56,2... | collective-permute-start | bytes 1572872 | tf_op jit(solution)/shard_map/ppermute | solution.py:30
  37.3 29.8 %collective-permute-start.22 = (bf16[4,4,2,64,128]{4,3,2,1,0:T(8,128)(2,1)S(1)}, bf16[4,4,2,64,128]{4,3,2,1,0:T(8,128)(2,1)S(1)}, u32[]{:S(2)}, u32[]{:S(2)}) collective-permute-start(bf16[4,4,2,64,128]{4,3,2,1,0:T(8,128)(2,1)S(1)} %pad_maximum_fusion), channel_id=1, source_target_pairs={{0,64},{8,72},{16,80},{24,88},{32,96},{40,104},{48,112},{56,120},{... | collective-permute-start | bytes 1572872 | tf_op jit(solution)/shard_map/ppermute | solution.py:30
  40.7 19.7 %collective-permute-start.7 = (bf16[3,4,2,64,128]{4,3,2,1,0:T(8,128)(2,1)S(1)}, bf16[3,4,2,64,128]{4,3,2,1,0:T(8,128)(2,1)S(1)}, u32[]{:S(2)}, u32[]{:S(2)}) collective-permute-start(bf16[3,4,2,64,128]{4,3,2,1,0:T(8,128)(2,1)S(1)} %pad_maximum_fusion.1), channel_id=1, source_target_pairs={{0,56},{8,0},{16,8},{24,16},{32,24},{40,32},{48,40},{56,48},{64,12... | collective-permute-start | bytes 1179656 | tf_op jit(solution)/shard_map/ppermute | solution.py:30
  44.9 15.6 %collective-permute-start.18 = (bf16[2,4,2,64,128]{4,3,2,1,0:T(8,128)(2,1)S(1)}, bf16[2,4,2,64,128]{4,3,2,1,0:T(8,128)(2,1)S(1)}, u32[]{:S(2)}, u32[]{:S(2)}) collective-permute-start(bf16[2,4,2,64,128]{4,3,2,1,0:T(8,128)(2,1)S(1)} %collective-permute-done.17.refs_6_), channel_id=1, source_target_pairs={{0,56},{8,0},{16,8},{24,16},{32,24},{40,32},{48,40},{56,48},{64,12... | collective-permute-start | bytes 786440 | tf_op jit(solution)/shard_map/ppermute | solution.py:30
  44.9 16.7 %collective-permute-start.4 = (bf16[3,4,2,64,128]{4,3,2,1,0:T(8,128)(2,1)S(1)}, bf16[3,4,2,64,128]{4,3,2,1,0:T(8,128)(2,1)S(1)}, u32[]{:S(2)}, u32[]{:S(2)}) collective-permute-start(bf16[3,4,2,64,128]{4,3,2,1,0:T(8,128)(2,1)S(1)} %collective-permute-done.3.refs_1_), channel_id=1, source_target_pairs={{0,8},{8,16},{16,24},{24,32},{32,40},{40,48},{48,56},{56,0},{64,72... | collective-permute-start | bytes 1179656 | tf_op jit(solution)/shard_map/ppermute | solution.py:30
  60.4 9.9 %collective-permute-start.8 = (bf16[3,4,2,64,128]{4,3,2,1,0:T(8,128)(2,1)S(1)}, bf16[3,4,2,64,128]{4,3,2,1,0:T(8,128)(2,1)S(1)}, u32[]{:S(2)}, u32[]{:S(2)}) collective-permute-start(bf16[3,4,2,64,128]{4,3,2,1,0:T(8,128)(2,1)S(1)} %collective-permute-done.7.refs_4_), channel_id=1, source_target_pairs={{0,56},{8,0},{16,8},{24,16},{32,24},{40,32},{48,40},{56,48},{64,12... | collective-permute-start | bytes 1179656 | tf_op jit(solution)/shard_map/ppermute | solution.py:30
  60.6 9.9 %collective-permute-start.19 = (bf16[3,4,2,64,128]{4,3,2,1,0:T(8,128)(2,1)S(1)}, bf16[3,4,2,64,128]{4,3,2,1,0:T(8,128)(2,1)S(1)}, u32[]{:S(2)}, u32[]{:S(2)}) collective-permute-start(bf16[3,4,2,64,128]{4,3,2,1,0:T(8,128)(2,1)S(1)} %pad_maximum_fusion.2), channel_id=1, source_target_pairs={{0,64},{8,72},{16,80},{24,88},{32,96},{40,104},{48,112},{56,120},{... | collective-permute-start | bytes 1179656 | tf_op jit(solution)/shard_map/ppermute | solution.py:30
  61.6 9.9 %collective-permute-start.5 = (bf16[3,4,2,64,128]{4,3,2,1,0:T(8,128)(2,1)S(1)}, bf16[3,4,2,64,128]{4,3,2,1,0:T(8,128)(2,1)S(1)}, u32[]{:S(2)}, u32[]{:S(2)}) collective-permute-start(bf16[3,4,2,64,128]{4,3,2,1,0:T(8,128)(2,1)S(1)} %collective-permute-done.4.refs_2_), channel_id=1, source_target_pairs={{0,8},{8,16},{16,24},{24,32},{32,40},{40,48},{48,56},{56,0},{64,72... | collective-permute-start | bytes 1179656 | tf_op jit(solution)/shard_map/ppermute | solution.py:30
  64.8 19.3 %collective-permute-start.15 = (bf16[4,4,2,64,128]{4,3,2,1,0:T(8,128)(2,1)S(1)}, bf16[4,4,2,64,128]{4,3,2,1,0:T(8,128)(2,1)S(1)}, u32[]{:S(2)}, u32[]{:S(2)}) collective-permute-start(bf16[4,4,2,64,128]{4,3,2,1,0:T(8,128)(2,1)S(1)} %collective-permute-done.14.refs_7_), channel_id=1, source_target_pairs={{0,192},{8,200},{16,208},{24,216},{32,224},{40,232},{48,240},{56,2... | collective-permute-start | bytes 1572872 | tf_op jit(solution)/shard_map/ppermute | solution.py:30
  67.1 17.0 %collective-permute-start.21 = (bf16[3,4,2,64,128]{4,3,2,1,0:T(8,128)(2,1)S(1)}, bf16[3,4,2,64,128]{4,3,2,1,0:T(8,128)(2,1)S(1)}, u32[]{:S(2)}, u32[]{:S(2)}) collective-permute-start(bf16[3,4,2,64,128]{4,3,2,1,0:T(8,128)(2,1)S(1)} %pad_maximum_fusion.2), channel_id=1, source_target_pairs={{0,192},{8,200},{16,208},{24,216},{32,224},{40,232},{48,240},{56,2... | collective-permute-start | bytes 1179656 | tf_op jit(solution)/shard_map/ppermute | solution.py:30
  70.3 13.8 %collective-permute-start.9 = (bf16[3,4,2,64,128]{4,3,2,1,0:T(8,128)(2,1)S(1)}, bf16[3,4,2,64,128]{4,3,2,1,0:T(8,128)(2,1)S(1)}, u32[]{:S(2)}, u32[]{:S(2)}) collective-permute-start(bf16[3,4,2,64,128]{4,3,2,1,0:T(8,128)(2,1)S(1)} %collective-permute-done.8.refs_5_), channel_id=1, source_target_pairs={{0,56},{8,0},{16,8},{24,16},{32,24},{40,32},{48,40},{56,48},{64,12... | collective-permute-start | bytes 1179656 | tf_op jit(solution)/shard_map/ppermute | solution.py:30
  70.5 13.6 %collective-permute-start.20 = (bf16[3,4,2,64,128]{4,3,2,1,0:T(8,128)(2,1)S(1)}, bf16[3,4,2,64,128]{4,3,2,1,0:T(8,128)(2,1)S(1)}, u32[]{:S(2)}, u32[]{:S(2)}) collective-permute-start(bf16[3,4,2,64,128]{4,3,2,1,0:T(8,128)(2,1)S(1)} %collective-permute-done.19.refs_8_), channel_id=1, source_target_pairs={{0,64},{8,72},{16,80},{24,88},{32,96},{40,104},{48,112},{56,120},{... | collective-permute-start | bytes 1179656 | tf_op jit(solution)/shard_map/ppermute | solution.py:30
  71.5 12.6 %collective-permute-start.6 = (bf16[3,4,2,64,128]{4,3,2,1,0:T(8,128)(2,1)S(1)}, bf16[3,4,2,64,128]{4,3,2,1,0:T(8,128)(2,1)S(1)}, u32[]{:S(2)}, u32[]{:S(2)}) collective-permute-start(bf16[3,4,2,64,128]{4,3,2,1,0:T(8,128)(2,1)S(1)} %collective-permute-done.5.refs_3_), channel_id=1, source_target_pairs={{0,8},{8,16},{16,24},{24,32},{32,40},{40,48},{48,56},{56,0},{64,72... | collective-permute-start | bytes 1179656 | tf_op jit(solution)/shard_map/ppermute | solution.py:30
where the time goes:
time: 93.2 us; the launch traced here: 93.6 us
  starting transfers between devices  33.2 us (36%)
  Pallas kernels  29.4 us (32%)
  waiting for transfers between devices  17.4 us (19%)
  blocking collectives  11.9 us (13%)
  other arithmetic  1.18 us (1%)
    ppermute x23, starting transfers between devices, moved(): return lax.ppermute(block, 'ctx', route)  33.2 us
    pallas_call x3, Pallas kernels, attend(): pl.pallas_call(functools.partial(attend_kernel, places, not state, closin...  29.4 us
    ppermute x23, waiting for transfers between devices, moved(): return lax.ppermute(block, 'ctx', route)  17.4 us
    all_to_all x1, blocking collectives, on_device(): lax.all_to_all(jnp.concatenate([keys, values]), 'tp', split_axis=1, conca...  11.9 us
  transfers between devices with their start and end apart: 23, of which 8 were waited for; matrix products, arithmetic and copies ran while one was open for 0% of the time, Pallas kernels for 21%

commit v1 on v0

--- a/solution.py
+++ b/solution.py
@@ -195,9 +195,19 @@
             fetch(bufs[0].at[0], qb, slot).wait()
 
         if opening:
+            odd = (cnt[qb] - 1) % 2
             arrived(0)
-            step([0], [block], True, True)
-            base = 1
+
+            @pl.when(odd == 0)
+            def _():
+                step([0], [block], True, True)
+
+            @pl.when(odd == 1)
+            def _():
+                arrived(1)
+                step([0, 1], [block, lid[qb, 1]], True, True)
+
+            base = 1 + odd
         else:
             base = 0
         seen = cnt[qb] - base
@@ -218,11 +228,13 @@
             def _():
                 step(slots, ids, False, False)
 
-        @pl.when(seen % 2 == 1)
-        def _():
-            last = base + seen - 1
-            arrived(last)
-            step([last], [lid[qb, last]], True, False)
+        if not opening:
+
+            @pl.when(seen % 2 == 1)
+            def _():
+                last = base + seen - 1
+                arrived(last)
+                step([last], [lid[qb, last]], True, False)
 
         if closing:
             for h in range(GROUP):

time: 93.2 us -> 95.4 us (1.024)
  the two profiles are of different devices: /device:TPU:96 before, /device:TPU:102 now
where the time goes in v1:
time: 95.4 us; the launch traced here: 94.4 us
  starting transfers between devices  40.6 us (43%)
  Pallas kernels  26.8 us (28%)
  waiting for transfers between devices  13.4 us (14%)
  blocking collectives  11.9 us (12%)
  other arithmetic  1.18 us (1%)
    ppermute x23, starting transfers between devices, moved(): return lax.ppermute(block, 'ctx', route)  40.6 us
    pallas_call x3, Pallas kernels, attend(): pl.pallas_call(functools.partial(attend_kernel, places, not state, closin...  26.8 us
    ppermute x23, waiting for transfers between devices, moved(): return lax.ppermute(block, 'ctx', route)  13.4 us
    all_to_all x1, blocking collectives, on_device(): lax.all_to_all(jnp.concatenate([keys, values]), 'tp', split_axis=1, conca...  11.9 us
  transfers between devices with their start and end apart: 23, of which 5 were waited for; matrix products, arithmetic and copies ran while one was open for 0% of the time, Pallas kernels for 18%

profile of v1, /device:TPU:102, one launch (start us, length us, event | category | flops | bytes accessed | tf_op | source)
XLA Modules:
  0.0 94.4 jit_solution(14636133306366762944)
XLA Ops:
  0.0 1.0 %copy_bitcast_fusion = bf16[128,8,128]{2,0,1:T(8,128)(2,1)S(1)} fusion(bf16[64,1024]{1,0:T(8,128)(2,1)} %param.9, bf16[64,1024]{1,0:T(8,128)(2,1)} %param.8), kind=kLoop, calls=%fused_computation.3 | loop fusion | flops 524288 | bytes 524288 | tf_op jit(solution)/shard_map/all_to_all | solution.py:290
  1.0 0.0 copy-start
  1.0 0.0 copy-start.1
  1.0 0.0 copy-start.2
  1.1 11.9 %all_to_all.16 = bf16[128,8,128]{2,0,1:T(8,128)(2,1)S(1)} all-to-all(bf16[128,8,128]{2,0,1:T(8,128)(2,1)S(1)} %copy_bitcast_fusion), channel_id=1, replica_groups=mesh['ctx'=32,'tp'=8] {'tp'}, dimensions={1} | all-to-all | bytes 524288 | tf_op jit(solution)/shard_map/all_to_all | solution.py:290
  13.0 0.5 collective-permute-start
  13.5 0.1 collective-permute-start.11
  13.6 3.1 %collective-permute-start.10 = (bf16[2,4,2,64,128]{4,3,2,1,0:T(8,128)(2,1)S(1)}, bf16[2,4,2,64,128]{4,3,2,1,0:T(8,128)(2,1)S(1)}, u32[]{:S(2)}, u32[]{:S(2)}) collective-permute-start(bf16[2,4,2,64,128]{4,3,2,1,0:T(8,128)(2,1)S(1)} %bitcast.10), channel_id=1, source_target_pairs={{0,8},{8,16},{16,24},{24,32},{32,40},{40,48},{48,56},{56,0},{64,72... | collective-permute-start | bytes 786440 | tf_op jit(solution)/shard_map/ppermute | solution.py:30
  16.7 1.5 %collective-permute-start.1 = (bf16[2,4,2,64,128]{4,3,2,1,0:T(8,128)(2,1)S(1)}, bf16[2,4,2,64,128]{4,3,2,1,0:T(8,128)(2,1)S(1)}, u32[]{:S(2)}, u32[]{:S(2)}) collective-permute-start(bf16[2,4,2,64,128]{4,3,2,1,0:T(8,128)(2,1)S(1)} %bitcast.11), channel_id=1, source_target_pairs={{0,192},{8,200},{16,208},{24,216},{32,224},{40,232},{48,240},{56,2... | collective-permute-start | bytes 786440 | tf_op jit(solution)/shard_map/ppermute | solution.py:30
  18.3 2.4 %collective-permute-done.refs_7_ = bf16[2,4,2,64,128]{4,3,2,1,0:T(8,128)(2,1)S(1)} collective-permute-done((bf16[2,4,2,64,128]{4,3,2,1,0:T(8,128)(2,1)S(1)}, bf16[2,4,2,64,128]{4,3,2,1,0:T(8,128)(2,1)S(1)}, u32[]{:S(2)}, u32[]{:S(2)}) %collective-permute-start) | collective-permute-done | bytes 262176 | tf_op jit(solution)/shard_map/ppermute | solution.py:30
  20.7 1.7 %collective-permute-start.2 = (bf16[2,4,2,64,128]{4,3,2,1,0:T(8,128)(2,1)S(1)}, bf16[2,4,2,64,128]{4,3,2,1,0:T(8,128)(2,1)S(1)}, u32[]{:S(2)}, u32[]{:S(2)}) collective-permute-start(bf16[2,4,2,64,128]{4,3,2,1,0:T(8,128)(2,1)S(1)} %collective-permute-done.refs_7_), channel_id=1, source_target_pairs={{0,64},{8,72},{16,80},{24,88},{32,96},{40,104},{48,112},{56,120},{... | collective-permute-start | bytes 786440 | tf_op jit(solution)/shard_map/ppermute | solution.py:30
  22.4 0.0 collective-permute-done.11.refs_4_
  22.4 0.1 collective-permute-start.13
  22.5 0.0 collective-permute-done.10.refs_1_
  22.5 3.1 %collective-permute-start.12 = (bf16[2,4,2,64,128]{4,3,2,1,0:T(8,128)(2,1)S(1)}, bf16[2,4,2,64,128]{4,3,2,1,0:T(8,128)(2,1)S(1)}, u32[]{:S(2)}, u32[]{:S(2)}) collective-permute-start(bf16[2,4,2,64,128]{4,3,2,1,0:T(8,128)(2,1)S(1)} %collective-permute-done.10.refs_1_), channel_id=1, source_target_pairs={{0,8},{8,16},{16,24},{24,32},{32,40},{40,48},{48,56},{56,0},{64,72... | collective-permute-start | bytes 786440 | tf_op jit(solution)/shard_map/ppermute | solution.py:30
  25.7 1.8 %collective-permute-done.2.refs_8_ = bf16[2,4,2,64,128]{4,3,2,1,0:T(8,128)(2,1)S(1)} collective-permute-done((bf16[2,4,2,64,128]{4,3,2,1,0:T(8,128)(2,1)S(1)}, bf16[2,4,2,64,128]{4,3,2,1,0:T(8,128)(2,1)S(1)}, u32[]{:S(2)}, u32[]{:S(2)}) %collective-permute-start.2) | collective-permute-done | bytes 262176 | tf_op jit(solution)/shard_map/ppermute | solution.py:30
  27.5 3.2 %collective-permute-start.3 = (bf16[3,4,2,64,128]{4,3,2,1,0:T(8,128)(2,1)S(1)}, bf16[3,4,2,64,128]{4,3,2,1,0:T(8,128)(2,1)S(1)}, u32[]{:S(2)}, u32[]{:S(2)}) collective-permute-start(bf16[3,4,2,64,128]{4,3,2,1,0:T(8,128)(2,1)S(1)} %pad_maximum_fusion.1), channel_id=1, source_target_pairs={{0,8},{8,16},{16,24},{24,32},{32,40},{40,48},{48,56},{56,0},{64,72... | collective-permute-start | bytes 1179656 | tf_op jit(solution)/shard_map/ppermute | solution.py:30
  30.7 0.0 collective-permute-done.13.refs_5_
  30.7 0.0 collective-permute-start.17
  30.7 0.0 collective-permute-done.12.refs_2_
  30.7 3.6 %collective-permute-start.16 = (bf16[2,4,2,64,128]{4,3,2,1,0:T(8,128)(2,1)S(1)}, bf16[2,4,2,64,128]{4,3,2,1,0:T(8,128)(2,1)S(1)}, u32[]{:S(2)}, u32[]{:S(2)}) collective-permute-start(bf16[2,4,2,64,128]{4,3,2,1,0:T(8,128)(2,1)S(1)} %collective-permute-done.12.refs_2_), channel_id=1, source_target_pairs={{0,8},{8,16},{16,24},{24,32},{32,40},{40,48},{48,56},{56,0},{64,72... | collective-permute-start | bytes 786440 | tf_op jit(solution)/shard_map/ppermute | solution.py:30
  34.4 0.1 pad_maximum_fusion
  34.5 2.0 %collective-permute-start.14 = (bf16[4,4,2,64,128]{4,3,2,1,0:T(8,128)(2,1)S(1)}, bf16[4,4,2,64,128]{4,3,2,1,0:T(8,128)(2,1)S(1)}, u32[]{:S(2)}, u32[]{:S(2)}) collective-permute-start(bf16[4,4,2,64,128]{4,3,2,1,0:T(8,128)(2,1)S(1)} %pad_maximum_fusion), channel_id=1, source_target_pairs={{0,192},{8,200},{16,208},{24,216},{32,224},{40,232},{48,240},{56,2... | collective-permute-start | bytes 1572872 | tf_op jit(solution)/shard_map/ppermute | solution.py:30
  36.5 1.3 %collective-permute-start.22 = (bf16[4,4,2,64,128]{4,3,2,1,0:T(8,128)(2,1)S(1)}, bf16[4,4,2,64,128]{4,3,2,1,0:T(8,128)(2,1)S(1)}, u32[]{:S(2)}, u32[]{:S(2)}) collective-permute-start(bf16[4,4,2,64,128]{4,3,2,1,0:T(8,128)(2,1)S(1)} %pad_maximum_fusion), channel_id=1, source_target_pairs={{0,64},{8,72},{16,80},{24,88},{32,96},{40,104},{48,112},{56,120},{... | collective-permute-start | bytes 1572872 | tf_op jit(solution)/shard_map/ppermute | solution.py:30
  37.8 0.5 collective-permute-done.17.refs_6_
  38.3 0.0 collective-permute-start.7
  38.3 5.3 %collective-permute-done.16.refs_3_ = bf16[2,4,2,64,128]{4,3,2,1,0:T(8,128)(2,1)S(1)} collective-permute-done((bf16[2,4,2,64,128]{4,3,2,1,0:T(8,128)(2,1)S(1)}, bf16[2,4,2,64,128]{4,3,2,1,0:T(8,128)(2,1)S(1)}, u32[]{:S(2)}, u32[]{:S(2)}) %collective-permute-start.16) | collective-permute-done | bytes 262176 | tf_op jit(solution)/shard_map/ppermute | solution.py:30
  43.6 0.2 collective-permute-start.18
  43.8 0.0 collective-permute-done.3.refs_1_
  43.8 3.5 %collective-permute-start.4 = (bf16[3,4,2,64,128]{4,3,2,1,0:T(8,128)(2,1)S(1)}, bf16[3,4,2,64,128]{4,3,2,1,0:T(8,128)(2,1)S(1)}, u32[]{:S(2)}, u32[]{:S(2)}) collective-permute-start(bf16[3,4,2,64,128]{4,3,2,1,0:T(8,128)(2,1)S(1)} %collective-permute-done.3.refs_1_), channel_id=1, source_target_pairs={{0,8},{8,16},{16,24},{24,32},{32,40},{40,48},{48,56},{56,0},{64,72... | collective-permute-start | bytes 1179656 | tf_op jit(solution)/shard_map/ppermute | solution.py:30
  47.3 9.1 %shard_map.55 = (s32[68]{0:T(128)S(1)}, f32[16,256,128]{2,1,0:T(8,128)S(1)}, f32[16,256,128]{2,1,0:T(8,128)S(1)}, f32[16,256,128]{2,1,0:T(8,128)S(1)}) custom-call(s32[64]{0:T(128)S(1)} %copy-done.1, s32[64]{0:T(128)S(1)} %copy-done.2, bf16[512,1024]{1,0:T(8,128)(2,1)S(1)} %copy-done, bf16[2,4,2,64,128]{4,3,2,1,0:T(8,128)(2,1)S(1)} %bitcast.12, ...), custom_call_target="tpu_custom_call" | custom-call | flops 6000000000 | bytes 8388608 | tf_op jit(solution)/shard_map/pallas_call | solution.py:263
  56.5 0.1 collective-permute-start.8
  56.6 0.0 collective-permute-done.18.refs_0_
  56.7 1.3 %collective-permute-start.19 = (bf16[3,4,2,64,128]{4,3,2,1,0:T(8,128)(2,1)S(1)}, bf16[3,4,2,64,128]{4,3,2,1,0:T(8,128)(2,1)S(1)}, u32[]{:S(2)}, u32[]{:S(2)}) collective-permute-start(bf16[3,4,2,64,128]{4,3,2,1,0:T(8,128)(2,1)S(1)} %pad_maximum_fusion.2), channel_id=1, source_target_pairs={{0,64},{8,72},{16,80},{24,88},{32,96},{40,104},{48,112},{56,120},{... | collective-permute-start | bytes 1179656 | tf_op jit(solution)/shard_map/ppermute | solution.py:30
  57.9 3.0 %collective-permute-start.5 = (bf16[3,4,2,64,128]{4,3,2,1,0:T(8,128)(2,1)S(1)}, bf16[3,4,2,64,128]{4,3,2,1,0:T(8,128)(2,1)S(1)}, u32[]{:S(2)}, u32[]{:S(2)}) collective-permute-start(bf16[3,4,2,64,128]{4,3,2,1,0:T(8,128)(2,1)S(1)} %collective-permute-done.4.refs_2_), channel_id=1, source_target_pairs={{0,8},{8,16},{16,24},{24,32},{32,40},{40,48},{48,56},{56,0},{64,72... | collective-permute-start | bytes 1179656 | tf_op jit(solution)/shard_map/ppermute | solution.py:30
  61.0 0.0 collective-permute-done.14.refs_7_
  61.0 1.0 %collective-permute-start.15 = (bf16[4,4,2,64,128]{4,3,2,1,0:T(8,128)(2,1)S(1)}, bf16[4,4,2,64,128]{4,3,2,1,0:T(8,128)(2,1)S(1)}, u32[]{:S(2)}, u32[]{:S(2)}) collective-permute-start(bf16[4,4,2,64,128]{4,3,2,1,0:T(8,128)(2,1)S(1)} %collective-permute-done.14.refs_7_), channel_id=1, source_target_pairs={{0,192},{8,200},{16,208},{24,216},{32,224},{40,232},{48,240},{56,2... | collective-permute-start | bytes 1572872 | tf_op jit(solution)/shard_map/ppermute | solution.py:30
  62.0 4.5 %collective-permute-start.21 = (bf16[3,4,2,64,128]{4,3,2,1,0:T(8,128)(2,1)S(1)}, bf16[3,4,2,64,128]{4,3,2,1,0:T(8,128)(2,1)S(1)}, u32[]{:S(2)}, u32[]{:S(2)}) collective-permute-start(bf16[3,4,2,64,128]{4,3,2,1,0:T(8,128)(2,1)S(1)} %pad_maximum_fusion.2), channel_id=1, source_target_pairs={{0,192},{8,200},{16,208},{24,216},{32,224},{40,232},{48,240},{56,2... | collective-permute-start | bytes 1179656 | tf_op jit(solution)/shard_map/ppermute | solution.py:30
  66.5 0.0 collective-permute-done.8.refs_5_
  66.5 0.1 collective-permute-start.9
  66.6 3.6 %collective-permute-start.20 = (bf16[3,4,2,64,128]{4,3,2,1,0:T(8,128)(2,1)S(1)}, bf16[3,4,2,64,128]{4,3,2,1,0:T(8,128)(2,1)S(1)}, u32[]{:S(2)}, u32[]{:S(2)}) collective-permute-start(bf16[3,4,2,64,128]{4,3,2,1,0:T(8,128)(2,1)S(1)} %collective-permute-done.19.refs_8_), channel_id=1, source_target_pairs={{0,64},{8,72},{16,80},{24,88},{32,96},{40,104},{48,112},{56,120},{... | collective-permute-start | bytes 1179656 | tf_op jit(solution)/shard_map/ppermute | solution.py:30
  70.2 0.0 collective-permute-done.5.refs_3_
  70.2 2.9 %collective-permute-start.6 = (bf16[3,4,2,64,128]{4,3,2,1,0:T(8,128)(2,1)S(1)}, bf16[3,4,2,64,128]{4,3,2,1,0:T(8,128)(2,1)S(1)}, u32[]{:S(2)}, u32[]{:S(2)}) collective-permute-start(bf16[3,4,2,64,128]{4,3,2,1,0:T(8,128)(2,1)S(1)} %collective-permute-done.5.refs_3_), channel_id=1, source_target_pairs={{0,8},{8,16},{16,24},{24,32},{32,40},{40,48},{48,56},{56,0},{64,72... | collective-permute-start | bytes 1179656 | tf_op jit(solution)/shard_map/ppermute | solution.py:30
  73.2 8.0 %shard_map.56 = (f32[16,256,128]{2,1,0:T(8,128)S(1)}, f32[16,256,128]{2,1,0:T(8,128)S(1)}, f32[16,256,128]{2,1,0:T(8,128)S(1)}) custom-call(s32[64]{0:T(128)S(1)} %copy-done.1, s32[64]{0:T(128)S(1)} %copy-done.2, bf16[512,1024]{1,0:T(8,128)(2,1)S(1)} %copy-done, ...), custom_call_target="tpu_custom_call", output_to_operand_aliasing={{0}: (13, {}), {1}: (14, {}), {2}: (15, {})} | custom-call | flops 8400000000 | bytes 8388608 | tf_op jit(solution)/shard_map/pallas_call | solution.py:263
  81.2 3.4 %collective-permute-done.21.refs_4_ = bf16[3,4,2,64,128]{4,3,2,1,0:T(8,128)(2,1)S(1)} collective-permute-done((bf16[3,4,2,64,128]{4,3,2,1,0:T(8,128)(2,1)S(1)}, bf16[3,4,2,64,128]{4,3,2,1,0:T(8,128)(2,1)S(1)}, u32[]{:S(2)}, u32[]{:S(2)}) %collective-permute-start.21) | collective-permute-done | bytes 393248 | tf_op jit(solution)/shard_map/ppermute | solution.py:30
  84.6 0.0 collective-permute-done.9.refs_1_
  84.6 0.0 collective-permute-done.20.refs_3_
  84.6 9.6 %shard_map.57 = (f32[16,256,128]{2,1,0:T(8,128)S(1)}, f32[16,256,128]{2,1,0:T(8,128)S(1)}, f32[16,256,128]{2,1,0:T(8,128)S(1)}, bf16[512,1024]{1,0:T(8,128)(2,1)}) custom-call(s32[64]{0:T(128)S(1)} %copy-done.1, s32[64]{0:T(128)S(1)} %copy-done.2, bf16[512,1024]{1,0:T(8,128)(2,1)S(1)} %copy-done, ...), custom_call_target="tpu_custom_call", output_to_operand_aliasing={{0}: (9, {}), {1}: (10, {}), {2}: (11, {})} | custom-call | flops 4800000000 | bytes 8388608 | tf_op jit(solution)/shard_map/pallas_call | solution.py:263
  (22 shorter events, 0.2 us)
Async XLA Ops:
  1.0 46.3 %copy-start = (bf16[512,1024]{1,0:T(8,128)(2,1)S(1)}, bf16[512,1024]{1,0:T(8,128)(2,1)}, u32[]{:S(2)}) copy-start(bf16[512,1024]{1,0:T(8,128)(2,1)} %q_ref.5) | copy-start | bytes 3145732
  1.0 46.3 %copy-start.1 = (s32[64]{0:T(128)S(1)}, s32[64]{0:T(128)}, u32[]{:S(2)}) copy-start(s32[64]{0:T(128)} %home_ref.5) | copy-start | bytes 772
  1.0 46.3 %copy-start.2 = (s32[64]{0:T(128)S(1)}, s32[64]{0:T(128)}, u32[]{:S(2)}) copy-start(s32[64]{0:T(128)} %bound_ref.5) | copy-start | bytes 772
  13.0 7.7 %collective-permute-start = (bf16[2,4,2,64,128]{4,3,2,1,0:T(8,128)(2,1)S(1)}, bf16[2,4,2,64,128]{4,3,2,1,0:T(8,128)(2,1)S(1)}, u32[]{:S(2)}, u32[]{:S(2)}) collective-permute-start(bf16[2,4,2,64,128]{4,3,2,1,0:T(8,128)(2,1)S(1)} %bitcast.8), channel_id=1, source_target_pairs={{0,64},{8,72},{16,80},{24,88},{32,96},{40,104},{48,112},{56,120},{... | collective-permute-start | bytes 786440 | tf_op jit(solution)/shard_map/ppermute | solution.py:30
  13.5 8.9 %collective-permute-start.11 = (bf16[2,4,2,64,128]{4,3,2,1,0:T(8,128)(2,1)S(1)}, bf16[2,4,2,64,128]{4,3,2,1,0:T(8,128)(2,1)S(1)}, u32[]{:S(2)}, u32[]{:S(2)}) collective-permute-start(bf16[2,4,2,64,128]{4,3,2,1,0:T(8,128)(2,1)S(1)} %bitcast.9), channel_id=1, source_target_pairs={{0,56},{8,0},{16,8},{24,16},{32,24},{40,32},{48,40},{56,48},{64,12... | collective-permute-start | bytes 786440 | tf_op jit(solution)/shard_map/ppermute | solution.py:30
  13.6 8.9 %collective-permute-start.10 = (bf16[2,4,2,64,128]{4,3,2,1,0:T(8,128)(2,1)S(1)}, bf16[2,4,2,64,128]{4,3,2,1,0:T(8,128)(2,1)S(1)}, u32[]{:S(2)}, u32[]{:S(2)}) collective-permute-start(bf16[2,4,2,64,128]{4,3,2,1,0:T(8,128)(2,1)S(1)} %bitcast.10), channel_id=1, source_target_pairs={{0,8},{8,16},{16,24},{24,32},{32,40},{40,48},{48,56},{56,0},{64,72... | collective-permute-start | bytes 786440 | tf_op jit(solution)/shard_map/ppermute | solution.py:30
  16.7 8.9 %collective-permute-start.1 = (bf16[2,4,2,64,128]{4,3,2,1,0:T(8,128)(2,1)S(1)}, bf16[2,4,2,64,128]{4,3,2,1,0:T(8,128)(2,1)S(1)}, u32[]{:S(2)}, u32[]{:S(2)}) collective-permute-start(bf16[2,4,2,64,128]{4,3,2,1,0:T(8,128)(2,1)S(1)} %bitcast.11), channel_id=1, source_target_pairs={{0,192},{8,200},{16,208},{24,216},{32,224},{40,232},{48,240},{56,2... | collective-permute-start | bytes 786440 | tf_op jit(solution)/shard_map/ppermute | solution.py:30
  20.7 6.8 %collective-permute-start.2 = (bf16[2,4,2,64,128]{4,3,2,1,0:T(8,128)(2,1)S(1)}, bf16[2,4,2,64,128]{4,3,2,1,0:T(8,128)(2,1)S(1)}, u32[]{:S(2)}, u32[]{:S(2)}) collective-permute-start(bf16[2,4,2,64,128]{4,3,2,1,0:T(8,128)(2,1)S(1)} %collective-permute-done.refs_7_), channel_id=1, source_target_pairs={{0,64},{8,72},{16,80},{24,88},{32,96},{40,104},{48,112},{56,120},{... | collective-permute-start | bytes 786440 | tf_op jit(solution)/shard_map/ppermute | solution.py:30
  22.4 8.3 %collective-permute-start.13 = (bf16[2,4,2,64,128]{4,3,2,1,0:T(8,128)(2,1)S(1)}, bf16[2,4,2,64,128]{4,3,2,1,0:T(8,128)(2,1)S(1)}, u32[]{:S(2)}, u32[]{:S(2)}) collective-permute-start(bf16[2,4,2,64,128]{4,3,2,1,0:T(8,128)(2,1)S(1)} %collective-permute-done.11.refs_4_), channel_id=1, source_target_pairs={{0,56},{8,0},{16,8},{24,16},{32,24},{40,32},{48,40},{56,48},{64,12... | collective-permute-start | bytes 786440 | tf_op jit(solution)/shard_map/ppermute | solution.py:30
  22.5 8.2 %collective-permute-start.12 = (bf16[2,4,2,64,128]{4,3,2,1,0:T(8,128)(2,1)S(1)}, bf16[2,4,2,64,128]{4,3,2,1,0:T(8,128)(2,1)S(1)}, u32[]{:S(2)}, u32[]{:S(2)}) collective-permute-start(bf16[2,4,2,64,128]{4,3,2,1,0:T(8,128)(2,1)S(1)} %collective-permute-done.10.refs_1_), channel_id=1, source_target_pairs={{0,8},{8,16},{16,24},{24,32},{32,40},{40,48},{48,56},{56,0},{64,72... | collective-permute-start | bytes 786440 | tf_op jit(solution)/shard_map/ppermute | solution.py:30
  27.5 16.3 %collective-permute-start.3 = (bf16[3,4,2,64,128]{4,3,2,1,0:T(8,128)(2,1)S(1)}, bf16[3,4,2,64,128]{4,3,2,1,0:T(8,128)(2,1)S(1)}, u32[]{:S(2)}, u32[]{:S(2)}) collective-permute-start(bf16[3,4,2,64,128]{4,3,2,1,0:T(8,128)(2,1)S(1)} %pad_maximum_fusion.1), channel_id=1, source_target_pairs={{0,8},{8,16},{16,24},{24,32},{32,40},{40,48},{48,56},{56,0},{64,72... | collective-permute-start | bytes 1179656 | tf_op jit(solution)/shard_map/ppermute | solution.py:30
  30.7 7.6 %collective-permute-start.17 = (bf16[2,4,2,64,128]{4,3,2,1,0:T(8,128)(2,1)S(1)}, bf16[2,4,2,64,128]{4,3,2,1,0:T(8,128)(2,1)S(1)}, u32[]{:S(2)}, u32[]{:S(2)}) collective-permute-start(bf16[2,4,2,64,128]{4,3,2,1,0:T(8,128)(2,1)S(1)} %collective-permute-done.13.refs_5_), channel_id=1, source_target_pairs={{0,56},{8,0},{16,8},{24,16},{32,24},{40,32},{48,40},{56,48},{64,12... | collective-permute-start | bytes 786440 | tf_op jit(solution)/shard_map/ppermute | solution.py:30
  30.7 12.9 %collective-permute-start.16 = (bf16[2,4,2,64,128]{4,3,2,1,0:T(8,128)(2,1)S(1)}, bf16[2,4,2,64,128]{4,3,2,1,0:T(8,128)(2,1)S(1)}, u32[]{:S(2)}, u32[]{:S(2)}) collective-permute-start(bf16[2,4,2,64,128]{4,3,2,1,0:T(8,128)(2,1)S(1)} %collective-permute-done.12.refs_2_), channel_id=1, source_target_pairs={{0,8},{8,16},{16,24},{24,32},{32,40},{40,48},{48,56},{56,0},{64,72... | collective-permute-start | bytes 786440 | tf_op jit(solution)/shard_map/ppermute | solution.py:30
  34.5 26.5 %collective-permute-start.14 = (bf16[4,4,2,64,128]{4,3,2,1,0:T(8,128)(2,1)S(1)}, bf16[4,4,2,64,128]{4,3,2,1,0:T(8,128)(2,1)S(1)}, u32[]{:S(2)}, u32[]{:S(2)}) collective-permute-start(bf16[4,4,2,64,128]{4,3,2,1,0:T(8,128)(2,1)S(1)} %pad_maximum_fusion), channel_id=1, source_target_pairs={{0,192},{8,200},{16,208},{24,216},{32,224},{40,232},{48,240},{56,2... | collective-permute-start | bytes 1572872 | tf_op jit(solution)/shard_map/ppermute | solution.py:30
  36.5 25.5 %collective-permute-start.22 = (bf16[4,4,2,64,128]{4,3,2,1,0:T(8,128)(2,1)S(1)}, bf16[4,4,2,64,128]{4,3,2,1,0:T(8,128)(2,1)S(1)}, u32[]{:S(2)}, u32[]{:S(2)}) collective-permute-start(bf16[4,4,2,64,128]{4,3,2,1,0:T(8,128)(2,1)S(1)} %pad_maximum_fusion), channel_id=1, source_target_pairs={{0,64},{8,72},{16,80},{24,88},{32,96},{40,104},{48,112},{56,120},{... | collective-permute-start | bytes 1572872 | tf_op jit(solution)/shard_map/ppermute | solution.py:30
  38.3 18.2 %collective-permute-start.7 = (bf16[3,4,2,64,128]{4,3,2,1,0:T(8,128)(2,1)S(1)}, bf16[3,4,2,64,128]{4,3,2,1,0:T(8,128)(2,1)S(1)}, u32[]{:S(2)}, u32[]{:S(2)}) collective-permute-start(bf16[3,4,2,64,128]{4,3,2,1,0:T(8,128)(2,1)S(1)} %pad_maximum_fusion.1), channel_id=1, source_target_pairs={{0,56},{8,0},{16,8},{24,16},{32,24},{40,32},{48,40},{56,48},{64,12... | collective-permute-start | bytes 1179656 | tf_op jit(solution)/shard_map/ppermute | solution.py:30
  43.6 13.0 %collective-permute-start.18 = (bf16[2,4,2,64,128]{4,3,2,1,0:T(8,128)(2,1)S(1)}, bf16[2,4,2,64,128]{4,3,2,1,0:T(8,128)(2,1)S(1)}, u32[]{:S(2)}, u32[]{:S(2)}) collective-permute-start(bf16[2,4,2,64,128]{4,3,2,1,0:T(8,128)(2,1)S(1)} %collective-permute-done.17.refs_6_), channel_id=1, source_target_pairs={{0,56},{8,0},{16,8},{24,16},{32,24},{40,32},{48,40},{56,48},{64,12... | collective-permute-start | bytes 786440 | tf_op jit(solution)/shard_map/ppermute | solution.py:30
  43.8 14.1 %collective-permute-start.4 = (bf16[3,4,2,64,128]{4,3,2,1,0:T(8,128)(2,1)S(1)}, bf16[3,4,2,64,128]{4,3,2,1,0:T(8,128)(2,1)S(1)}, u32[]{:S(2)}, u32[]{:S(2)}) collective-permute-start(bf16[3,4,2,64,128]{4,3,2,1,0:T(8,128)(2,1)S(1)} %collective-permute-done.3.refs_1_), channel_id=1, source_target_pairs={{0,8},{8,16},{16,24},{24,32},{32,40},{40,48},{48,56},{56,0},{64,72... | collective-permute-start | bytes 1179656 | tf_op jit(solution)/shard_map/ppermute | solution.py:30
  56.5 10.0 %collective-permute-start.8 = (bf16[3,4,2,64,128]{4,3,2,1,0:T(8,128)(2,1)S(1)}, bf16[3,4,2,64,128]{4,3,2,1,0:T(8,128)(2,1)S(1)}, u32[]{:S(2)}, u32[]{:S(2)}) collective-permute-start(bf16[3,4,2,64,128]{4,3,2,1,0:T(8,128)(2,1)S(1)} %collective-permute-done.7.refs_4_), channel_id=1, source_target_pairs={{0,56},{8,0},{16,8},{24,16},{32,24},{40,32},{48,40},{56,48},{64,12... | collective-permute-start | bytes 1179656 | tf_op jit(solution)/shard_map/ppermute | solution.py:30
  56.7 9.9 %collective-permute-start.19 = (bf16[3,4,2,64,128]{4,3,2,1,0:T(8,128)(2,1)S(1)}, bf16[3,4,2,64,128]{4,3,2,1,0:T(8,128)(2,1)S(1)}, u32[]{:S(2)}, u32[]{:S(2)}) collective-permute-start(bf16[3,4,2,64,128]{4,3,2,1,0:T(8,128)(2,1)S(1)} %pad_maximum_fusion.2), channel_id=1, source_target_pairs={{0,64},{8,72},{16,80},{24,88},{32,96},{40,104},{48,112},{56,120},{... | collective-permute-start | bytes 1179656 | tf_op jit(solution)/shard_map/ppermute | solution.py:30
  57.9 12.3 %collective-permute-start.5 = (bf16[3,4,2,64,128]{4,3,2,1,0:T(8,128)(2,1)S(1)}, bf16[3,4,2,64,128]{4,3,2,1,0:T(8,128)(2,1)S(1)}, u32[]{:S(2)}, u32[]{:S(2)}) collective-permute-start(bf16[3,4,2,64,128]{4,3,2,1,0:T(8,128)(2,1)S(1)} %collective-permute-done.4.refs_2_), channel_id=1, source_target_pairs={{0,8},{8,16},{16,24},{24,32},{32,40},{40,48},{48,56},{56,0},{64,72... | collective-permute-start | bytes 1179656 | tf_op jit(solution)/shard_map/ppermute | solution.py:30
  61.0 23.6 %collective-permute-start.15 = (bf16[4,4,2,64,128]{4,3,2,1,0:T(8,128)(2,1)S(1)}, bf16[4,4,2,64,128]{4,3,2,1,0:T(8,128)(2,1)S(1)}, u32[]{:S(2)}, u32[]{:S(2)}) collective-permute-start(bf16[4,4,2,64,128]{4,3,2,1,0:T(8,128)(2,1)S(1)} %collective-permute-done.14.refs_7_), channel_id=1, source_target_pairs={{0,192},{8,200},{16,208},{24,216},{32,224},{40,232},{48,240},{56,2... | collective-permute-start | bytes 1572872 | tf_op jit(solution)/shard_map/ppermute | solution.py:30
  62.0 22.6 %collective-permute-start.21 = (bf16[3,4,2,64,128]{4,3,2,1,0:T(8,128)(2,1)S(1)}, bf16[3,4,2,64,128]{4,3,2,1,0:T(8,128)(2,1)S(1)}, u32[]{:S(2)}, u32[]{:S(2)}) collective-permute-start(bf16[3,4,2,64,128]{4,3,2,1,0:T(8,128)(2,1)S(1)} %pad_maximum_fusion.2), channel_id=1, source_target_pairs={{0,192},{8,200},{16,208},{24,216},{32,224},{40,232},{48,240},{56,2... | collective-permute-start | bytes 1179656 | tf_op jit(solution)/shard_map/ppermute | solution.py:30
  66.5 18.0 %collective-permute-start.9 = (bf16[3,4,2,64,128]{4,3,2,1,0:T(8,128)(2,1)S(1)}, bf16[3,4,2,64,128]{4,3,2,1,0:T(8,128)(2,1)S(1)}, u32[]{:S(2)}, u32[]{:S(2)}) collective-permute-start(bf16[3,4,2,64,128]{4,3,2,1,0:T(8,128)(2,1)S(1)} %collective-permute-done.8.refs_5_), channel_id=1, source_target_pairs={{0,56},{8,0},{16,8},{24,16},{32,24},{40,32},{48,40},{56,48},{64,12... | collective-permute-start | bytes 1179656 | tf_op jit(solution)/shard_map/ppermute | solution.py:30
  66.6 18.0 %collective-permute-start.20 = (bf16[3,4,2,64,128]{4,3,2,1,0:T(8,128)(2,1)S(1)}, bf16[3,4,2,64,128]{4,3,2,1,0:T(8,128)(2,1)S(1)}, u32[]{:S(2)}, u32[]{:S(2)}) collective-permute-start(bf16[3,4,2,64,128]{4,3,2,1,0:T(8,128)(2,1)S(1)} %collective-permute-done.19.refs_8_), channel_id=1, source_target_pairs={{0,64},{8,72},{16,80},{24,88},{32,96},{40,104},{48,112},{56,120},{... | collective-permute-start | bytes 1179656 | tf_op jit(solution)/shard_map/ppermute | solution.py:30
  70.2 14.4 %collective-permute-start.6 = (bf16[3,4,2,64,128]{4,3,2,1,0:T(8,128)(2,1)S(1)}, bf16[3,4,2,64,128]{4,3,2,1,0:T(8,128)(2,1)S(1)}, u32[]{:S(2)}, u32[]{:S(2)}) collective-permute-start(bf16[3,4,2,64,128]{4,3,2,1,0:T(8,128)(2,1)S(1)} %collective-permute-done.5.refs_3_), channel_id=1, source_target_pairs={{0,8},{8,16},{16,24},{24,32},{32,40},{40,48},{48,56},{56,0},{64,72... | collective-permute-start | bytes 1179656 | tf_op jit(solution)/shard_map/ppermute | solution.py:30
